TPU v7x, 32 devices: a whole 2x2x4 slice. The times are simulated.
32 devices in a mesh: gx: 4 (over x, core), gy: 2 (over y), gz: 4 (over z).
Axes of the slice: x: 2, y: 2, z: 4, core: 2. Of those that a mesh axis runs over, the one named last changes fastest.
Arguments:
- right_side: float32 [128, 32, 512], P('gx', 'gy', 'gz'), may hold values from -6 to 6
- phase_label: int32 [128, 32, 512], P('gx', 'gy', 'gz'), may hold values from 0 to 2
- viscosity: float32 [128, 32, 512], P('gx', 'gy', 'gz'), may hold values from 0.5 to 4
- mobility_table: float32 [3], replicated, may hold values from 0.05 to 2
- shift_table: float32 [3], replicated, may hold values from 0.0005 to 0.004
Outputs:
- correction: float32 [128, 32, 512], P('gx', 'gy', 'gz')
All inputs are finite; a program needn't handle non-finite values.
Results may differ from a plain program's by a relative error of at most 0.00002.
Values sent between devices are 32-bit elements; how exact they have to be, the bound alone decides.
A program may use at most 128 MiB of HBM per device.

v0:
```python
import jax
import jax.numpy as jnp
from jax import lax
from jax.sharding import PartitionSpec as P

LEVELS = 5
COARSE_SWEEPS = 48


OMEGA = 0.8


def extended(value, sides, width):
    for axis, dim in sides:
        peers, length = (lax.axis_size(axis), value.shape[dim])
        up = [(i, (i + 1) % peers) for i in range(peers - 1)]
        down = [(j, i) for i, j in up]
        last = lax.slice_in_dim(value, length - width, length, axis=dim)
        leading = lax.slice_in_dim(value, 0, width, axis=dim)
        before = lax.ppermute(last, axis, up)
        after = lax.ppermute(leading, axis, down)
        value = jnp.concatenate([before, value, after], axis=dim)
    return value


def harmonic(first, second):
    return 2.0 * first * second / (first + second)


def neighbours(padded):
    return [
        padded[2:, 1:-1, 1:-1],
        padded[:-2, 1:-1, 1:-1],
        padded[1:-1, 2:, 1:-1],
        padded[1:-1, :-2, 1:-1],
        padded[1:-1, 1:-1, 2:],
        padded[1:-1, 1:-1, :-2],
    ]


def face_terms(padded, mobility):
    return [harmonic(mobility, other) for other in neighbours(padded)]


def operate(padded, field, terms, shift):
    total = shift * field
    for term, other in zip(terms, neighbours(padded)):
        total = total + term * (field - other)
    return total


def diagonal_of(terms, shift):
    total = shift
    for term in terms:
        total = total + term
    return total


def block_sum(field):
    a, b, c = field.shape
    return field.reshape(a // 2, 2, b // 2, 2, c // 2, 2).sum(axis=(1, 3, 5))


def spread(field):
    return jnp.repeat(jnp.repeat(jnp.repeat(field, 2, 0), 2, 1), 2, 2)


def remote_terms(mobility):
    padded = extended(mobility, (("gx", 0), ("gy", 1), ("gz", 2)), 1)
    return face_terms(padded, mobility)


def remote_apply(field, terms, shift):
    padded = extended(field, (("gx", 0), ("gy", 1), ("gz", 2)), 1)
    return operate(padded, field, terms, shift)


def coarse_solve(rhs, mobility, shift):
    terms = face_terms(jnp.pad(mobility, 1), mobility)
    diag = diagonal_of(terms, shift)
    start = OMEGA * rhs / diag

    def sweep(step, field):
        return field + OMEGA * (rhs - operate(jnp.pad(field, 1), field, terms, shift)) / diag

    return lax.fori_loop(0, COARSE_SWEEPS - 1, sweep, start)


def whole_cycle(rhs, mobility, shift):
    return coarse_solve(rhs, mobility, shift)


def collected(rhs, mobility, shift):
    local_a, local_b, local_c = rhs.shape
    stacked = jnp.stack([rhs, mobility, shift])
    whole = lax.all_gather(stacked, "gz", axis=3, tiled=True)
    whole = lax.all_gather(whole, "gy", axis=2, tiled=True)
    whole = lax.all_gather(whole, "gx", axis=1, tiled=True)
    solved = whole_cycle(whole[0], whole[1], whole[2])
    begin_x = lax.axis_index("gx") * local_a
    begin_y = lax.axis_index("gy") * local_b
    begin_z = lax.axis_index("gz") * local_c
    return lax.dynamic_slice(solved, (begin_x, begin_y, begin_z), (local_a, local_b, local_c))


def cycle(level, rhs, mobility, shift, joined_level):
    if level == joined_level:
        return collected(rhs, mobility, shift)
    terms = remote_terms(mobility)
    diag = diagonal_of(terms, shift)
    field = OMEGA * rhs / diag
    field = field + OMEGA * (rhs - remote_apply(field, terms, shift)) / diag
    remain = rhs - remote_apply(field, terms, shift)
    coarse = cycle(
        level + 1, block_sum(remain), block_sum(mobility) / 4.0, block_sum(shift), joined_level
    )
    field = field + spread(coarse)
    for sweep_index in range(2):
        field = field + OMEGA * (rhs - remote_apply(field, terms, shift)) / diag
    return field


def body(right_side, phase_label, viscosity, mobility_table, shift_table):
    mobility = mobility_table[phase_label] / viscosity
    shift = shift_table[phase_label]
    joined_level = LEVELS - 1
    return cycle(0, right_side, mobility, shift, joined_level)


def solution(mesh):
    in_specs = (P("gx", "gy", "gz"), P("gx", "gy", "gz"), P("gx", "gy", "gz"), P(), P())
    out_specs = P("gx", "gy", "gz")
    return jax.shard_map(body, mesh=mesh, in_specs=in_specs, out_specs=out_specs, check_vma=False)
```

profile of v0, /device:TPU:0, one launch (start us, length us, event | category | flops | bytes accessed | tf_op | source)
XLA Modules:
  0.0 616.2 jit_solution(1983936433589788973)
XLA Ops:
  6.4 4.8 select_select_fusion
  15.6 18.1 %reshape.93 = f32[16,2,8,2,64,2]{5,4,3,2,1,0:T(8,128)} reshape(f32[32,16,128]{2,1,0:T(8,128)S(1)} %get-tuple-element.274) | data formatting | bytes 524288 | tf_op jit(solution)/shard_map/reshape | solution.py:61
  33.7 7.0 %reduce_sum.125 = f32[16,8,64]{2,1,0:T(8,128)S(1)} reduce(f32[16,2,8,2,64,2]{5,4,3,2,1,0:T(8,128)} %reshape.93, f32[]{:T(128)} %constant.62.clone.1), dimensions={1,3,5}, to_apply=%region_2.0 | reduce | flops 57344 | bytes 294916 | tf_op jit(solution)/shard_map/reduce_sum | solution.py:61
  42.0 5.1 collective-permute-start.19
  51.7 4.8 collective-permute-start.37
  60.1 18.1 %reshape.92 = f32[16,2,8,2,64,2]{5,4,3,2,1,0:T(8,128)} reshape(f32[32,16,128]{2,1,0:T(8,128)S(1)} %get-tuple-element.273) | data formatting | bytes 524288 | tf_op jit(solution)/shard_map/reshape | solution.py:61
  78.2 7.0 %reduce_sum.124 = f32[16,8,64]{2,1,0:T(8,128)S(1)} reduce(f32[16,2,8,2,64,2]{5,4,3,2,1,0:T(8,128)} %reshape.92, f32[]{:T(128)} %constant.62.clone.1), dimensions={1,3,5}, to_apply=%region_1.0 | reduce | flops 57344 | bytes 294916 | tf_op jit(solution)/shard_map/reduce_sum | solution.py:61
  96.1 6.7 %collective-permute-done.5 = f32[34,18,1]{2,0,1:T(8,128)S(1)} collective-permute-done((f32[34,18,1]{2,0,1:T(8,128)S(1)}, f32[34,18,1]{2,0,1:T(8,128)S(1)}, u32[]{:S(2)}, u32[]{:S(2)}) %collective-permute-start.5) | collective-permute-done | bytes 2480 | tf_op jit(solution)/shard_map/ppermute | solution.py:20
  133.0 4.9 collective-permute-done.10
  163.0 5.4 collective-permute-start.17
  168.5 5.1 collective-permute-done.16
  178.5 18.1 %reshape.91 = f32[16,2,8,2,64,2]{5,4,3,2,1,0:T(8,128)} reshape(f32[32,16,128]{2,1,0:T(8,128)S(1)} %fusion.59) | data formatting | bytes 524288 | tf_op jit(solution)/shard_map/reshape | solution.py:61
  196.6 7.0 %reduce_sum.123 = f32[16,8,64]{2,1,0:T(8,128)S(1)} reduce(f32[16,2,8,2,64,2]{5,4,3,2,1,0:T(8,128)} %reshape.91, f32[]{:T(128)} %constant.62.clone.1), dimensions={1,3,5}, to_apply=%region_0.0 | reduce | flops 57344 | bytes 294916 | tf_op jit(solution)/shard_map/reduce_sum | solution.py:61
  227.2 5.0 collective-permute-start.29
  238.0 4.9 collective-permute-start.31
  265.2 5.2 collective-permute-start.41
  313.6 5.1 collective-permute-start.53
  321.3 5.2 collective-permute-start.59
  353.5 4.8 collective-permute-start.67
  377.7 13.1 %all_gather.9 = f32[3,2,1,32]{0,1,2,3:T(2,128)S(1)} all-gather(f32[3,2,1,8]{0,1,2,3:T(2,128)S(1)} %copy.403), channel_id=1, replica_groups=mesh['gx'=4,'gy'=2,'gz'=4] {'gz'}, dimensions={3}, use_global_device_ids=true | all-gather | bytes 960 | tf_op jit(solution)/shard_map/all_gather | solution.py:96
  390.8 4.8 all_gather.10
  395.7 9.9 %all_gather.11 = f32[3,8,2,32]{3,2,0,1:T(2,128)S(1)} all-gather(f32[3,2,2,32]{3,2,0,1:T(2,128)S(1)} %copy.404), channel_id=1, replica_groups=mesh['gx'=4,'gy'=2,'gz'=4] {'gx'}, dimensions={1}, use_global_device_ids=true | all-gather | bytes 7680 | tf_op jit(solution)/shard_map/all_gather | solution.py:98
  405.7 5.9 while.12
  479.2 4.7 collective-permute-start.91
  529.2 5.0 collective-permute-start.103
  544.0 4.7 collective-permute-start.107
  554.7 5.0 collective-permute-start.109
  569.7 4.7 collective-permute-start.113
  574.4 5.0 collective-permute-done.112
  585.4 4.8 collective-permute-start.115
  599.9 4.7 collective-permute-start.119
  604.6 6.1 collective-permute-done.118
  (585 shorter events, 397.5 us)
Async XLA Ops:
  11.2 40.5 %collective-permute-start = (f32[1,16,128]{2,1,0:T(8,128)S(1)}, f32[1,16,128]{2,1,0:T(8,128)S(1)}, u32[]{:S(2)}, u32[]{:S(2)}) collective-permute-start(f32[1,16,128]{2,1,0:T(8,128)S(1)} %get-tuple-element.272), channel_id=1, source_target_pairs={{8,0},{16,8},{24,16},{9,1},{17,9},{25,17},{10,2},{18,10},{26,18},{... | collective-permute-start | bytes 24584 | tf_op jit(solution)/shard_map/ppermute | solution.py:21
  12.5 44.1 %collective-permute-start.1 = (f32[1,16,128]{2,1,0:T(8,128)S(1)}, f32[1,16,128]{2,1,0:T(8,128)S(1)}, u32[]{:S(2)}, u32[]{:S(2)}) collective-permute-start(f32[1,16,128]{2,1,0:T(8,128)S(1)} %get-tuple-element.271), channel_id=1, source_target_pairs={{0,8},{8,16},{16,24},{1,9},{9,17},{17,25},{2,10},{10,18},{18,26},{... | collective-permute-start | bytes 24584 | tf_op jit(solution)/shard_map/ppermute | solution.py:20
  40.7 54.0 %collective-permute-start.18 = (f32[1,8,64]{2,1,0:T(8,128)S(1)}, f32[1,8,64]{2,1,0:T(8,128)S(1)}, u32[]{:S(2)}, u32[]{:S(2)}) collective-permute-start(f32[1,8,64]{2,1,0:T(8,128)S(1)} %get-tuple-element.314), channel_id=1, source_target_pairs={{8,0},{16,8},{24,16},{9,1},{17,9},{25,17},{10,2},{18,10},{26,18},{... | collective-permute-start | bytes 6152 | tf_op jit(solution)/shard_map/ppermute | solution.py:21
  42.0 54.0 %collective-permute-start.19 = (f32[1,8,64]{2,1,0:T(8,128)S(1)}, f32[1,8,64]{2,1,0:T(8,128)S(1)}, u32[]{:S(2)}, u32[]{:S(2)}) collective-permute-start(f32[1,8,64]{2,1,0:T(8,128)S(1)} %get-tuple-element.313), channel_id=1, source_target_pairs={{0,8},{8,16},{16,24},{1,9},{9,17},{17,25},{2,10},{10,18},{18,26},{... | collective-permute-start | bytes 6152 | tf_op jit(solution)/shard_map/ppermute | solution.py:20
  50.1 187.9 %collective-permute-start.36 = (f32[1,4,32]{2,1,0:T(4,128)}, f32[1,4,32]{2,1,0:T(4,128)}, u32[]{:S(2)}, u32[]{:S(2)}) collective-permute-start(f32[1,4,32]{2,1,0:T(4,128)} %get-tuple-element.357), channel_id=1, source_target_pairs={{8,0},{16,8},{24,16},{9,1},{17,9},{25,17},{10,2},{18,10},{26,18},{... | collective-permute-start | bytes 1544 | tf_op jit(solution)/shard_map/ppermute | solution.py:21
  51.7 191.2 %collective-permute-start.37 = (f32[1,4,32]{2,1,0:T(4,128)}, f32[1,4,32]{2,1,0:T(4,128)}, u32[]{:S(2)}, u32[]{:S(2)}) collective-permute-start(f32[1,4,32]{2,1,0:T(4,128)} %get-tuple-element.356), channel_id=1, source_target_pairs={{0,8},{8,16},{16,24},{1,9},{9,17},{17,25},{2,10},{10,18},{18,26},{... | collective-permute-start | bytes 1544 | tf_op jit(solution)/shard_map/ppermute | solution.py:20
  56.6 28.6 %collective-permute-start.3 = (f32[34,1,128]{2,1,0:T(1,128)S(1)}, f32[34,1,128]{2,1,0:T(1,128)S(1)}, u32[]{:S(2)}, u32[]{:S(2)}) collective-permute-start(f32[34,1,128]{2,1,0:T(1,128)S(1)} %get-tuple-element.261), channel_id=1, source_target_pairs={{0,4},{1,5},{2,6},{3,7},{8,12},{9,13},{10,14},{11,15},{16,20},{17,... | collective-permute-start | bytes 52232 | tf_op jit(solution)/shard_map/ppermute | solution.py:20
  91.2 11.5 %collective-permute-start.5 = (f32[34,18,1]{2,0,1:T(8,128)S(1)}, f32[34,18,1]{2,0,1:T(8,128)S(1)}, u32[]{:S(2)}, u32[]{:S(2)}) collective-permute-start(f32[34,18,1]{2,0,1:T(8,128)S(1)} %get-tuple-element.251), channel_id=1, source_target_pairs={{0,1},{1,2},{2,3},{4,5},{5,6},{6,7},{8,9},{9,10},{10,11},{12,13},{... | collective-permute-start | bytes 7352 | tf_op jit(solution)/shard_map/ppermute | solution.py:20
  94.8 12.2 %collective-permute-start.4 = (f32[34,18,1]{2,0,1:T(8,128)S(1)}, f32[34,18,1]{2,0,1:T(8,128)S(1)}, u32[]{:S(2)}, u32[]{:S(2)}) collective-permute-start(f32[34,18,1]{2,0,1:T(8,128)S(1)} %get-tuple-element.252), channel_id=1, source_target_pairs={{1,0},{2,1},{3,2},{5,4},{6,5},{7,6},{9,8},{10,9},{11,10},{13,12},{... | collective-permute-start | bytes 7352 | tf_op jit(solution)/shard_map/ppermute | solution.py:21
  111.0 8.9 %collective-permute-start.7 = (f32[1,16,128]{2,1,0:T(8,128)S(1)}, f32[1,16,128]{2,1,0:T(8,128)S(1)}, u32[]{:S(2)}, u32[]{:S(2)}) collective-permute-start(f32[1,16,128]{2,1,0:T(8,128)S(1)} %get-tuple-element.269), channel_id=1, source_target_pairs={{0,8},{8,16},{16,24},{1,9},{9,17},{17,25},{2,10},{10,18},{18,26},{... | collective-permute-start | bytes 24584 | tf_op jit(solution)/shard_map/ppermute | solution.py:20
  114.0 33.2 %collective-permute-start.20 = (f32[18,1,64]{2,1,0:T(1,128)S(1)}, f32[18,1,64]{2,1,0:T(1,128)S(1)}, u32[]{:S(2)}, u32[]{:S(2)}) collective-permute-start(f32[18,1,64]{2,1,0:T(1,128)S(1)} %get-tuple-element.304), channel_id=1, source_target_pairs={{4,0},{5,1},{6,2},{7,3},{12,8},{13,9},{14,10},{15,11},{20,16},{21,... | collective-permute-start | bytes 13832 | tf_op jit(solution)/shard_map/ppermute | solution.py:21
  127.1 10.8 %collective-permute-start.10 = (f32[34,18,1]{2,0,1:T(8,128)S(1)}, f32[34,18,1]{2,0,1:T(8,128)S(1)}, u32[]{:S(2)}, u32[]{:S(2)}) collective-permute-start(f32[34,18,1]{2,0,1:T(8,128)S(1)} %get-tuple-element.247), channel_id=1, source_target_pairs={{1,0},{2,1},{3,2},{5,4},{6,5},{7,6},{9,8},{10,9},{11,10},{13,12},{... | collective-permute-start | bytes 7352 | tf_op jit(solution)/shard_map/ppermute | solution.py:21
  128.4 10.7 %collective-permute-start.11 = (f32[34,18,1]{2,0,1:T(8,128)S(1)}, f32[34,18,1]{2,0,1:T(8,128)S(1)}, u32[]{:S(2)}, u32[]{:S(2)}) collective-permute-start(f32[34,18,1]{2,0,1:T(8,128)S(1)} %get-tuple-element.248), channel_id=1, source_target_pairs={{0,1},{1,2},{2,3},{4,5},{5,6},{6,7},{8,9},{9,10},{10,11},{12,13},{... | collective-permute-start | bytes 7352 | tf_op jit(solution)/shard_map/ppermute | solution.py:20
  150.1 12.8 %collective-permute-start.23 = (f32[18,10,1]{2,0,1:T(8,128)S(1)}, f32[18,10,1]{2,0,1:T(8,128)S(1)}, u32[]{:S(2)}, u32[]{:S(2)}) collective-permute-start(f32[18,10,1]{2,0,1:T(8,128)S(1)} %get-tuple-element.293), channel_id=1, source_target_pairs={{0,1},{1,2},{2,3},{4,5},{5,6},{6,7},{8,9},{9,10},{10,11},{12,13},{... | collective-permute-start | bytes 2168 | tf_op jit(solution)/shard_map/ppermute | solution.py:20
  154.5 13.8 %collective-permute-start.22 = (f32[18,10,1]{2,0,1:T(8,128)S(1)}, f32[18,10,1]{2,0,1:T(8,128)S(1)}, u32[]{:S(2)}, u32[]{:S(2)}) collective-permute-start(f32[18,10,1]{2,0,1:T(8,128)S(1)} %get-tuple-element.294), channel_id=1, source_target_pairs={{1,0},{2,1},{3,2},{5,4},{6,5},{7,6},{9,8},{10,9},{11,10},{13,12},{... | collective-permute-start | bytes 2168 | tf_op jit(solution)/shard_map/ppermute | solution.py:21
  161.6 11.9 %collective-permute-start.16 = (f32[34,18,1]{2,0,1:T(8,128)S(1)}, f32[34,18,1]{2,0,1:T(8,128)S(1)}, u32[]{:S(2)}, u32[]{:S(2)}) collective-permute-start(f32[34,18,1]{2,0,1:T(8,128)S(1)} %get-tuple-element.243), channel_id=1, source_target_pairs={{1,0},{2,1},{3,2},{5,4},{6,5},{7,6},{9,8},{10,9},{11,10},{13,12},{... | collective-permute-start | bytes 7352 | tf_op jit(solution)/shard_map/ppermute | solution.py:21
  163.0 11.8 %collective-permute-start.17 = (f32[34,18,1]{2,0,1:T(8,128)S(1)}, f32[34,18,1]{2,0,1:T(8,128)S(1)}, u32[]{:S(2)}, u32[]{:S(2)}) collective-permute-start(f32[34,18,1]{2,0,1:T(8,128)S(1)} %get-tuple-element.244), channel_id=1, source_target_pairs={{0,1},{1,2},{2,3},{4,5},{5,6},{6,7},{8,9},{9,10},{10,11},{12,13},{... | collective-permute-start | bytes 7352 | tf_op jit(solution)/shard_map/ppermute | solution.py:20
  209.5 72.2 %collective-permute-start.54 = (f32[1,2,16]{2,0,1:T(1,128)}, f32[1,2,16]{2,0,1:T(1,128)}, u32[]{:S(2)}, u32[]{:S(2)}) collective-permute-start(f32[1,2,16]{2,0,1:T(1,128)} %get-tuple-element.379), channel_id=1, source_target_pairs={{8,0},{16,8},{24,16},{9,1},{17,9},{25,17},{10,2},{18,10},{26,18},{... | collective-permute-start | bytes 392 | tf_op jit(solution)/shard_map/ppermute | solution.py:21
  211.6 9.6 %collective-permute-start.27 = (f32[18,1,64]{2,1,0:T(1,128)}, f32[18,1,64]{2,1,0:T(1,128)}, u32[]{:S(2)}, u32[]{:S(2)}) collective-permute-start(f32[18,1,64]{2,1,0:T(1,128)} %get-tuple-element.302), channel_id=1, source_target_pairs={{0,4},{1,5},{2,6},{3,7},{8,12},{9,13},{10,14},{11,15},{16,20},{17,... | collective-permute-start | bytes 13832 | tf_op jit(solution)/shard_map/ppermute | solution.py:20
  233.4 48.3 %collective-permute-start.55 = (f32[1,2,16]{2,0,1:T(1,128)}, f32[1,2,16]{2,0,1:T(1,128)}, u32[]{:S(2)}, u32[]{:S(2)}) collective-permute-start(f32[1,2,16]{2,0,1:T(1,128)} %get-tuple-element.378), channel_id=1, source_target_pairs={{0,8},{8,16},{16,24},{1,9},{9,17},{17,25},{2,10},{10,18},{18,26},{... | collective-permute-start | bytes 392 | tf_op jit(solution)/shard_map/ppermute | solution.py:20
  238.0 11.6 %collective-permute-start.31 = (f32[1,8,64]{2,1,0:T(8,128)S(1)}, f32[1,8,64]{2,1,0:T(8,128)S(1)}, u32[]{:S(2)}, u32[]{:S(2)}) collective-permute-start(f32[1,8,64]{2,1,0:T(8,128)S(1)} %get-tuple-element.309), channel_id=1, source_target_pairs={{0,8},{8,16},{16,24},{1,9},{9,17},{17,25},{2,10},{10,18},{18,26},{... | collective-permute-start | bytes 6152 | tf_op jit(solution)/shard_map/ppermute | solution.py:20
  258.7 11.7 %collective-permute-start.35 = (f32[18,10,1]{2,0,1:T(8,128)S(1)}, f32[18,10,1]{2,0,1:T(8,128)S(1)}, u32[]{:S(2)}, u32[]{:S(2)}) collective-permute-start(f32[18,10,1]{2,0,1:T(8,128)S(1)} %get-tuple-element.286), channel_id=1, source_target_pairs={{0,1},{1,2},{2,3},{4,5},{5,6},{6,7},{8,9},{9,10},{10,11},{12,13},{... | collective-permute-start | bytes 2168 | tf_op jit(solution)/shard_map/ppermute | solution.py:20
  263.9 12.2 %collective-permute-start.40 = (f32[10,6,1]{2,1,0:T(8,128)}, f32[10,6,1]{2,1,0:T(8,128)}, u32[]{:S(2)}, u32[]{:S(2)}) collective-permute-start(f32[10,6,1]{2,1,0:T(8,128)} %get-tuple-element.324), channel_id=1, source_target_pairs={{1,0},{2,1},{3,2},{5,4},{6,5},{7,6},{9,8},{10,9},{11,10},{13,12},{... | collective-permute-start | bytes 728 | tf_op jit(solution)/shard_map/ppermute | solution.py:21
  265.2 10.9 %collective-permute-start.41 = (f32[10,6,1]{2,1,0:T(8,128)}, f32[10,6,1]{2,1,0:T(8,128)}, u32[]{:S(2)}, u32[]{:S(2)}) collective-permute-start(f32[10,6,1]{2,1,0:T(8,128)} %get-tuple-element.323), channel_id=1, source_target_pairs={{0,1},{1,2},{2,3},{4,5},{5,6},{6,7},{8,9},{9,10},{10,11},{12,13},{... | collective-permute-start | bytes 728 | tf_op jit(solution)/shard_map/ppermute | solution.py:20
  289.8 10.5 %collective-permute-start.47 = (f32[10,6,1]{2,1,0:T(8,128)S(1)}, f32[10,6,1]{2,1,0:T(8,128)S(1)}, u32[]{:S(2)}, u32[]{:S(2)}) collective-permute-start(f32[10,6,1]{2,1,0:T(8,128)S(1)} %get-tuple-element.322), channel_id=1, source_target_pairs={{0,1},{1,2},{2,3},{4,5},{5,6},{6,7},{8,9},{9,10},{10,11},{12,13},{... | collective-permute-start | bytes 728 | tf_op jit(solution)/shard_map/ppermute | solution.py:20
  294.4 11.1 %collective-permute-start.56 = (f32[6,1,16]{2,0,1:T(8,128)S(1)}, f32[6,1,16]{2,0,1:T(8,128)S(1)}, u32[]{:S(2)}, u32[]{:S(2)}) collective-permute-start(f32[6,1,16]{2,0,1:T(8,128)S(1)} %get-tuple-element.367), channel_id=1, source_target_pairs={{4,0},{5,1},{6,2},{7,3},{12,8},{13,9},{14,10},{15,11},{20,16},{21,... | collective-permute-start | bytes 1160 | tf_op jit(solution)/shard_map/ppermute | solution.py:21
  295.7 9.8 %collective-permute-start.57 = (f32[6,1,16]{2,0,1:T(8,128)S(1)}, f32[6,1,16]{2,0,1:T(8,128)S(1)}, u32[]{:S(2)}, u32[]{:S(2)}) collective-permute-start(f32[6,1,16]{2,0,1:T(8,128)S(1)} %get-tuple-element.366), channel_id=1, source_target_pairs={{0,4},{1,5},{2,6},{3,7},{8,12},{9,13},{10,14},{11,15},{16,20},{17,... | collective-permute-start | bytes 1160 | tf_op jit(solution)/shard_map/ppermute | solution.py:20
  313.6 12.9 %collective-permute-start.53 = (f32[10,6,1]{2,1,0:T(8,128)S(1)}, f32[10,6,1]{2,1,0:T(8,128)S(1)}, u32[]{:S(2)}, u32[]{:S(2)}) collective-permute-start(f32[10,6,1]{2,1,0:T(8,128)S(1)} %get-tuple-element.320), channel_id=1, source_target_pairs={{0,1},{1,2},{2,3},{4,5},{5,6},{6,7},{8,9},{9,10},{10,11},{12,13},{... | collective-permute-start | bytes 728 | tf_op jit(solution)/shard_map/ppermute | solution.py:20
  568.4 11.0 %collective-permute-start.112 = (f32[34,18,1]{2,0,1:T(8,128)S(1)}, f32[34,18,1]{2,0,1:T(8,128)S(1)}, u32[]{:S(2)}, u32[]{:S(2)}) collective-permute-start(f32[34,18,1]{2,0,1:T(8,128)S(1)} %get-tuple-element.239), channel_id=1, source_target_pairs={{1,0},{2,1},{3,2},{5,4},{6,5},{7,6},{9,8},{10,9},{11,10},{13,12},{... | collective-permute-start | bytes 7352 | tf_op jit(solution)/shard_map/ppermute | solution.py:21
  569.7 11.4 %collective-permute-start.113 = (f32[34,18,1]{2,0,1:T(8,128)S(1)}, f32[34,18,1]{2,0,1:T(8,128)S(1)}, u32[]{:S(2)}, u32[]{:S(2)}) collective-permute-start(f32[34,18,1]{2,0,1:T(8,128)S(1)} %get-tuple-element.240), channel_id=1, source_target_pairs={{0,1},{1,2},{2,3},{4,5},{5,6},{6,7},{8,9},{9,10},{10,11},{12,13},{... | collective-permute-start | bytes 7352 | tf_op jit(solution)/shard_map/ppermute | solution.py:20
  598.6 12.2 %collective-permute-start.118 = (f32[34,18,1]{2,0,1:T(8,128)S(1)}, f32[34,18,1]{2,0,1:T(8,128)S(1)}, u32[]{:S(2)}, u32[]{:S(2)}) collective-permute-start(f32[34,18,1]{2,0,1:T(8,128)S(1)} %get-tuple-element.235), channel_id=1, source_target_pairs={{1,0},{2,1},{3,2},{5,4},{6,5},{7,6},{9,8},{10,9},{11,10},{13,12},{... | collective-permute-start | bytes 7352 | tf_op jit(solution)/shard_map/ppermute | solution.py:21
  599.9 12.6 %collective-permute-start.119 = (f32[34,18,1]{2,0,1:T(8,128)S(1)}, f32[34,18,1]{2,0,1:T(8,128)S(1)}, u32[]{:S(2)}, u32[]{:S(2)}) collective-permute-start(f32[34,18,1]{2,0,1:T(8,128)S(1)} %get-tuple-element.236), channel_id=1, source_target_pairs={{0,1},{1,2},{2,3},{4,5},{5,6},{6,7},{8,9},{9,10},{10,11},{12,13},{... | collective-permute-start | bytes 7352 | tf_op jit(solution)/shard_map/ppermute | solution.py:20
  (119 other events, 3147.3 us)
where the time goes:
time: 622 us; the launch traced here: 616 us
  starting transfers between devices  307 us (49%)
  waiting for transfers between devices  126 us (20%)
  local copies, waits for them, and re-layouts  76.2 us (12%)
  other arithmetic  75.5 us (12%)
  blocking collectives  27.8 us (4%)
    ppermute x60, starting transfers between devices, extended(): before = lax.ppermute(last, axis, up)  229 us
    ppermute x60, waiting for transfers between devices, extended(): after = lax.ppermute(leading, axis, down)  89.1 us
    ppermute x60, starting transfers between devices, extended(): after = lax.ppermute(leading, axis, down)  77.7 us
    reshape x7, local copies, waits for them, and re-layouts, block_sum(): return field.reshape(a // 2, 2, b // 2, 2, c // 2, 2).sum(axis=(1, 3, 5))  59.8 us
    ppermute x60, waiting for transfers between devices, extended(): before = lax.ppermute(last, axis, up)  36.7 us
    reduce_sum x18, other arithmetic, block_sum(): return field.reshape(a // 2, 2, b // 2, 2, c // 2, 2).sum(axis=(1, 3, 5))  28.8 us
    add x12, other arithmetic, cycle(): field = field + OMEGA * (rhs - remote_apply(field, terms, shift)) / diag  18 us
    all_gather x1, blocking collectives, collected(): whole = lax.all_gather(stacked, 'gz', axis=3, tiled=True)  13.1 us
  transfers between devices with their start and end apart: 120, of which 63 were waited for; matrix products, arithmetic and copies ran while one was open for 19% of the time, Pallas kernels for 0%

commit v1 on v0

v1 whole, which is shorter than its diff:
```python
import functools
import jax
import jax.numpy as jnp
from jax import lax
from jax.sharding import PartitionSpec as P
from jax.experimental import pallas as pl
from jax.experimental.pallas import tpu as pltpu

LEVELS = 5
COARSE_SWEEPS = 48
OMEGA = 0.8
LANES = 128
CHUNK = 8
MESH = pl.DeviceIdType.MESH


def dot(a, b):
    return jnp.dot(a, b, precision=lax.Precision.HIGHEST, preferred_element_type=jnp.float32)


def iota(shape, dim):
    return lax.broadcasted_iota(jnp.int32, shape, dim)


def ones_where(mask):
    return jnp.where(mask, 1.0, 0.0).astype(jnp.float32)


def pair_lanes(fine, coarse, zf, zc):
    i, j = iota((fine, coarse), 0), iota((fine, coarse), 1)
    return ones_where(((i // zf) // 2 == j // zc) & ((i % zf) // 2 == j % zc))


def pair_lanes_back(coarse, fine, zf, zc):
    j, i = iota((coarse, fine), 0), iota((coarse, fine), 1)
    return ones_where(((i // zf) // 2 == j // zc) & ((i % zf) // 2 == j % zc))


def kernel(sizes, b_ref, ph_ref, visc_ref, mt_ref, st_ref, out_ref,
           xa0, xb0, w0, inv0, dg0, zh0, sy0, sz0, rx0, ry0, rz0,
           xa1, xb1, w1, inv1, dg1, zh1, sy1, sz1, rx1, ry1, rz1,
           s0, base0, base1, r0, r1, m1, s1, t256, t128, t64,
           pk_ms, pk_r, g_ms, g_r, x2, wj2, wj3, dj2, dj3,
           ss, rs, gsem):
    GX, GY, GZ = sizes
    N = GX * GY * GZ
    ix, iy, iz = lax.axis_index("gx"), lax.axis_index("gy"), lax.axis_index("gz")
    me = (ix * GY + iy) * GZ + iz
    axes = ((ix, GX), (iy, GY), (iz, GZ))
    L0 = dict(n=(32, 16, 128), w=w0, inv=inv0, dg=dg0, zh=zh0, sy=sy0, sz=sz0, r=(rx0, ry0, rz0), off=0, base=base0)
    L1 = dict(n=(16, 8, 64), w=w1, inv=inv1, dg=dg1, zh=zh1, sy=sy1, sz=sz1, r=(rx1, ry1, rz1), off=5, base=base1)

    def copies(L, xp, e):
        nx = L["n"][0]
        srcs = ((xp.at[1], xp.at[nx]), (L["sy"].at[0], L["sy"].at[1]), (L["sz"].at[0], L["sz"].at[1]))
        out = []
        for a in range(3):
            pos, count = axes[a]
            for side in range(2):
                to = [ix, iy, iz]
                to[a] = pos - 1 if side == 0 else pos + 1
                there = pos > 0 if side == 0 else pos < count - 1
                k = L["off"] + e
                out.append((there, pltpu.make_async_remote_copy(
                    src_ref=srcs[a][side], dst_ref=L["r"][a].at[e, 1 - side],
                    send_sem=ss.at[k, 2 * a + side], recv_sem=rs.at[k, 2 * a + 1 - side],
                    device_id=tuple(to), device_id_type=MESH), L["r"][a].at[e, side]))
        return out

    def start(L, xp, e):
        nx, ny, nz = L["n"]
        todo = copies(L, xp, e)

        def go(which):
            for there, copy, _ in which:
                @pl.when(there)
                def _(copy=copy):
                    copy.start()
        go(todo[0:2])
        for c in range(nx // CHUNK):
            v = xp[1 + c * CHUNK:1 + (c + 1) * CHUNK]
            L["sy"][0, c * CHUNK:(c + 1) * CHUNK, :] = v[:, 0, :]
            L["sy"][1, c * CHUNK:(c + 1) * CHUNK, :] = v[:, ny - 1, :]
        go(todo[2:4])
        per = LANES // ny
        for k in range(nx // per):
            t = xp[1 + k * per:1 + (k + 1) * per].reshape(LANES, LANES).T
            L["sz"][0, k:k + 1, :] = t[0:1, :]
            L["sz"][1, k:k + 1, :] = t[nz - 1:nz, :]
        go(todo[4:6])

    def finish(L, xp, e):
        nx, ny, nz = L["n"]
        todo = copies(L, xp, e)
        for a in range(3):
            for side in range(2):
                there, copy, slot = todo[2 * a + side]
                other = todo[2 * a + 1 - side][1]

                @pl.when(there)
                def _(copy=copy, other=other):
                    copy.wait_send()
                    other.wait_recv()

                @pl.when(jnp.logical_not(there))
                def _(slot=slot):
                    slot[...] = jnp.zeros(slot.shape, jnp.float32)
        rx, ry, rz = L["r"]
        xp[0] = rx[e, 0]
        xp[nx + 1] = rx[e, 1]
        per = LANES // ny
        row = iota((LANES, LANES), 0)
        for k in range(nx // per):
            low = jnp.broadcast_to(rz[e, 0, k:k + 1, :], (LANES, LANES))
            high = jnp.broadcast_to(rz[e, 1, k:k + 1, :], (LANES, LANES))
            t = jnp.where(row == 0, low, jnp.where(row == nz - 1, high, 0.0)).T
            L["zh"][k * per:(k + 1) * per] = t.reshape(per, ny, LANES)

    def around(L, xp, e, i):
        nx, ny, nz = L["n"]
        shape = (CHUNK, ny, LANES)
        ry = L["r"][1]
        at = pl.multiple_of(i * CHUNK, CHUNK)
        v = xp[pl.ds(1 + at, CHUNK)]
        zh = L["zh"][pl.ds(at, CHUNK)]
        row, lane = iota(shape, 1), iota(shape, 2)
        low = jnp.broadcast_to(ry[e, 0, pl.ds(at, CHUNK), :][:, None, :], shape)
        high = jnp.broadcast_to(ry[e, 1, pl.ds(at, CHUNK), :][:, None, :], shape)
        return v, [xp[pl.ds(2 + at, CHUNK)], xp[pl.ds(at, CHUNK)],
                   jnp.where(row == ny - 1, high, pltpu.roll(v, ny - 1, 1)),
                   jnp.where(row == 0, low, pltpu.roll(v, 1, 1)),
                   jnp.where(lane == nz - 1, zh, pltpu.roll(v, LANES - 1, 2)),
                   jnp.where(lane == 0, zh, pltpu.roll(v, 1, 2))]

    def chunks(L, fn):
        def step(i, _):
            fn(i)
            return 0
        lax.fori_loop(0, L["n"][0] // CHUNK, step, 0)

    def coefficients(L, mp, e, s_ref):
        nx, ny, nz = L["n"]

        def one(i):
            at = pl.multiple_of(i * CHUNK, CHUNK)
            m, near = around(L, mp, e, i)
            valid = iota((CHUNK, ny, LANES), 2) < nz
            diag = s_ref[pl.ds(at, CHUNK)]
            terms = []
            for n in near:
                t = 2.0 * m * n / (m + n)
                if nz < LANES:
                    t = jnp.where(valid, t, 0.0)
                diag = diag + t
                terms.append(t)
            if nz < LANES:
                diag = jnp.where(valid, diag, 1.0)
            inv = OMEGA / diag
            L["inv"][pl.ds(at, CHUNK)] = inv
            L["dg"][pl.ds(at, CHUNK)] = diag * (1.0 / OMEGA)
            for d in range(6):
                L["w"][d, pl.ds(at, CHUNK)] = terms[d] * inv
        chunks(L, one)

    def begin(L, rhs, xp):
        def one(i):
            at = pl.multiple_of(i * CHUNK, CHUNK)
            v = rhs[pl.ds(at, CHUNK)] * L["inv"][pl.ds(at, CHUNK)]
            L["base"][pl.ds(at, CHUNK)] = v
            xp[pl.ds(1 + at, CHUNK)] = v
        chunks(L, one)

    def sweep(L, xp, e, put):
        def one(i):
            at = pl.multiple_of(i * CHUNK, CHUNK)
            v, near = around(L, xp, e, i)
            total = (1.0 - OMEGA) * v + L["base"][pl.ds(at, CHUNK)]
            for d in range(6):
                total = total + L["w"][d, pl.ds(at, CHUNK)] * near[d]
            put(at, v, total)
        chunks(L, one)

    def into(xp):
        def put(at, v, total):
            xp[pl.ds(1 + at, CHUNK)] = total
        return put

    def residual(L, r):
        def put(at, v, total):
            r[pl.ds(at, CHUNK)] = L["dg"][pl.ds(at, CHUNK)] * (total - v)
        return put

    def restrict0(load):
        halve = pair_lanes(LANES, LANES, LANES, 64)
        for c in range(2):
            v = load(c).reshape(8, 2, 16, LANES)
            v = v[:, 0] + v[:, 1]
            t256[c * 128:(c + 1) * 128, :] = dot(v.reshape(128, LANES), halve)
        return (t256[pl.ds(0, 128, stride=2), :] + t256[pl.ds(1, 128, stride=2), :]).reshape(16, 8, LANES)

    def pack(v):
        v = v.reshape(8, 2, 8, LANES)
        t64[...] = (v[:, 0] + v[:, 1]).reshape(64, LANES)
        total = jnp.zeros((8, LANES), jnp.float32)
        i, j = iota((LANES, LANES), 0), iota((LANES, LANES), 1)
        for q in range(4):
            place = ones_where((i < 64) & (j == 32 * q + i // 2))
            both = t64[pl.ds(2 * q, 8, stride=8), :] + t64[pl.ds(2 * q + 1, 8, stride=8), :]
            total = total + dot(both, place)
        return total

    def gather_start(src, dst, k):
        def send(step, _):
            peer = lax.rem(me + step, N)
            to = (peer // (GY * GZ), lax.rem(peer // GZ, GY), lax.rem(peer, GZ))
            pltpu.make_async_remote_copy(
                src_ref=src, dst_ref=dst.at[me], send_sem=gsem.at[2 * k], recv_sem=gsem.at[2 * k + 1],
                device_id=to, device_id_type=MESH).start()
            return 0
        lax.fori_loop(1, N, send, 0)

    def gather_finish(src, dst, k):
        rest = dst.at[pl.ds(0, N - 1)]
        pltpu.make_async_copy(rest, rest, gsem.at[2 * k]).wait()
        pltpu.make_async_copy(rest, rest, gsem.at[2 * k + 1]).wait()
        dst[pl.ds(me, 1)] = src[...][None]

    X2, Y2, Z2 = 8 * GX, 4 * GY, 32 * GZ

    def unpack(read):
        lane = iota((8, LANES), 1)
        rows = []
        for gx in range(GX):
            tiles = []
            for y in range(Y2):
                gy, q = y // 4, y % 4
                for t in range(Z2 // LANES):
                    tile = jnp.zeros((8, LANES), jnp.float32)
                    for p in range(4):
                        v = read((gx * GY + gy) * GZ + 4 * t + p)
                        shift = (32 * (p - q)) % LANES
                        v = pltpu.roll(v, shift, 1) if shift else v
                        tile = jnp.where(lane // 32 == p, v, tile)
                    tiles.append(tile)
            rows.append(jnp.concatenate(tiles, axis=1))
        return jnp.concatenate(rows, axis=0)

    def flat_terms(m, s, dims):
        X, Y, Z = dims
        shape = m.shape
        row, lane = iota(shape, 0), iota(shape, 1)
        width = shape[1]
        valid = lane < Y * Z
        z, y = lane % Z, lane // Z
        inside = [row < X - 1, row > 0, y < Y - 1, y > 0, z < Z - 1, z > 0]
        diag = s
        terms = []
        for near, ok in zip(flat_near(m, Z), inside):
            t = jnp.where(ok & valid, 2.0 * m * near / (m + near), 0.0)
            diag = diag + t
            terms.append(t)
        diag = jnp.where(valid, diag, 1.0)
        inv = OMEGA / diag
        return [t * inv for t in terms], inv, diag * (1.0 / OMEGA)

    def flat_near(v, Z):
        X, width = v.shape
        return [pltpu.roll(v, X - 1, 0), pltpu.roll(v, 1, 0),
                pltpu.roll(v, width - Z, 1), pltpu.roll(v, Z, 1),
                pltpu.roll(v, width - 1, 1), pltpu.roll(v, 1, 1)]

    def flat_sweep(v, base, w, Z):
        total = (1.0 - OMEGA) * v + base
        for d, near in enumerate(flat_near(v, Z)):
            total = total + w[d] * near
        return total

    def flat_restrict(r, dims):
        X, Y, Z = dims
        span = min(4 * LANES, Y * Z)
        place = pair_lanes(span, LANES, Z, Z // 2)
        tiles = [dot(r[:, k * span:(k + 1) * span], place) for k in range(Y * Z // span)]
        wide = jnp.concatenate(tiles, axis=1) if len(tiles) > 1 else tiles[0]
        left = ones_where(iota((X // 2, X), 1) // 2 == iota((X // 2, X), 0))
        return dot(left, wide)

    def flat_spread(e, dims):
        X, Y, Z = dims
        span = min(4 * LANES, Y * Z)
        left = ones_where(iota((X, X // 2), 0) // 2 == iota((X, X // 2), 1))
        tall = dot(left, e)
        place = pair_lanes_back(LANES, span, Z, Z // 2)
        tiles = [dot(tall[:, k * LANES:(k + 1) * LANES], place) for k in range(Y * Z // span)]
        return jnp.concatenate(tiles, axis=1) if len(tiles) > 1 else tiles[0]

    d2 = (X2, Y2, Z2)
    d3 = (X2 // 2, Y2 // 2, Z2 // 2)
    d4 = (X2 // 4, Y2 // 4, Z2 // 4)

    sz0[...] = jnp.zeros(sz0.shape, jnp.float32)
    sz1[...] = jnp.zeros(sz1.shape, jnp.float32)

    def look_up(i):
        at = pl.multiple_of(i * CHUNK, CHUNK)
        ph = ph_ref[pl.ds(at, CHUNK)]
        mob = jnp.full(ph.shape, mt_ref[0], jnp.float32)
        shift = jnp.full(ph.shape, st_ref[0], jnp.float32)
        for k in range(1, mt_ref.shape[0]):
            mob = jnp.where(ph == k, mt_ref[k], mob)
            shift = jnp.where(ph == k, st_ref[k], shift)
        xb0[pl.ds(1 + at, CHUNK)] = mob / visc_ref[pl.ds(at, CHUNK)]
        s0[pl.ds(at, CHUNK)] = shift
    chunks(L0, look_up)
    start(L0, xb0, 0)

    lane1 = iota((16, 8, LANES), 2)
    mob1 = restrict0(lambda c: xb0[1 + 16 * c:17 + 16 * c]) * 0.25
    xb1[1:17] = jnp.where(lane1 < 64, mob1, 1.0)
    start(L1, xb1, 0)
    s1[...] = restrict0(lambda c: s0[16 * c:16 + 16 * c])
    pk_ms[0:8, :] = pack(mob1) * 0.25
    pk_ms[8:16, :] = pack(s1[...])
    gather_start(pk_ms, g_ms, 0)

    finish(L0, xb0, 0)
    coefficients(L0, xb0, 0, s0)
    begin(L0, b_ref, xa0)
    start(L0, xa0, 1)
    finish(L1, xb1, 0)
    coefficients(L1, xb1, 0, s1)
    finish(L0, xa0, 1)
    sweep(L0, xa0, 1, into(xb0))
    start(L0, xb0, 2)

    gather_finish(pk_ms, g_ms, 0)
    m2 = unpack(lambda n: g_ms[n, 0:8, :])
    s2 = unpack(lambda n: g_ms[n, 8:16, :])
    w, inv, dg = flat_terms(m2, s2, d2)
    for d in range(6):
        wj2[d] = w[d]
    dj2[0], dj2[1] = inv, dg
    m3 = flat_restrict(m2, d2) * 0.25
    s3 = flat_restrict(s2, d2)
    w, inv, dg = flat_terms(m3, s3, d3)
    for d in range(6):
        wj3[d] = w[d]
    dj3[0], dj3[1] = inv, dg
    m4 = flat_restrict(m3, d3) * 0.25
    s4 = flat_restrict(s3, d3)
    w4, inv4, _ = flat_terms(m4, s4, d4)

    finish(L0, xb0, 2)
    sweep(L0, xb0, 2, residual(L0, r0))
    r1[...] = restrict0(lambda c: r0[16 * c:16 + 16 * c])
    begin(L1, r1, xa1)
    start(L1, xa1, 1)
    finish(L1, xa1, 1)
    sweep(L1, xa1, 1, into(xb1))
    start(L1, xb1, 2)
    finish(L1, xb1, 2)
    sweep(L1, xb1, 2, residual(L1, r1))
    pk_r[...] = pack(r1[...])
    gather_start(pk_r, g_r, 1)
    gather_finish(pk_r, g_r, 1)

    base2 = unpack(lambda n: g_r[n]) * dj2[0]
    w2 = [wj2.at[d] for d in range(6)]
    w3 = [wj3.at[d] for d in range(6)]

    def run(v, base, w, Z):
        return flat_sweep(v, base, [ref[...] for ref in w], Z)

    v2 = run(base2, base2, w2, Z2)
    b3 = flat_restrict(dj2[1] * (run(v2, base2, w2, Z2) - v2), d2)
    base3 = b3 * dj3[0]
    v3 = run(base3, base3, w3, Z2 // 2)
    b4 = flat_restrict(dj3[1] * (run(v3, base3, w3, Z2 // 2) - v3), d3)
    base4 = b4 * inv4
    v4 = lax.fori_loop(0, COARSE_SWEEPS - 1, lambda _, v: flat_sweep(v, base4, w4, Z2 // 4), base4)
    v3 = v3 + flat_spread(v4, d3)
    for _ in range(2):
        v3 = run(v3, base3, w3, Z2 // 2)
    v2 = v2 + flat_spread(v3, d2)
    for _ in range(2):
        v2 = run(v2, base2, w2, Z2)
    x2[...] = v2

    widen32 = ones_where((iota((LANES, LANES), 1) // 2 == iota((LANES, LANES), 0)) & (iota((LANES, LANES), 1) < 64))
    for q in range(4):
        column = pl.multiple_of((iy * 4 + q) * Z2 + (iz // 4) * LANES, LANES)
        tile = x2[pl.ds(pl.multiple_of(ix * 8, 8), 8), pl.ds(column, LANES)]
        tile = pltpu.roll(tile, lax.rem(LANES - 32 * lax.rem(iz, 4), LANES), 1)
        tile = dot(tile, widen32)
        t64[pl.ds(2 * q, 8, stride=8), :] = tile
        t64[pl.ds(2 * q + 1, 8, stride=8), :] = tile
    e1 = jnp.broadcast_to(t64[...].reshape(8, 1, 8, LANES), (8, 2, 8, LANES)).reshape(16, 8, LANES)
    xa1[1:17] = xb1[1:17] + e1
    start(L1, xa1, 3)
    finish(L1, xa1, 3)
    sweep(L1, xa1, 3, into(xb1))
    start(L1, xb1, 4)
    finish(L1, xb1, 4)
    sweep(L1, xb1, 4, into(xa1))

    widen64 = pair_lanes_back(LANES, LANES, LANES, 64)
    wide = dot(xa1[1:17].reshape(128, LANES), widen64)
    t256[pl.ds(0, 128, stride=2), :] = wide
    t256[pl.ds(1, 128, stride=2), :] = wide
    for c in range(16):
        e0 = t256[16 * c:16 * c + 16, :]
        xa0[1 + 2 * c] = xb0[1 + 2 * c] + e0
        xa0[2 + 2 * c] = xb0[2 + 2 * c] + e0
    start(L0, xa0, 3)
    finish(L0, xa0, 3)
    sweep(L0, xa0, 3, into(xb0))
    start(L0, xb0, 4)
    finish(L0, xb0, 4)

    def put(at, v, total):
        out_ref[pl.ds(at, CHUNK)] = total
    sweep(L0, xb0, 4, put)


def body(sizes, right_side, phase_label, viscosity, mobility_table, shift_table):
    GX, GY, GZ = sizes
    N = GX * GY * GZ
    f32 = jnp.float32
    V = lambda *shape: pltpu.VMEM(shape, f32)

    def level(nx, ny):
        return [V(nx + 2, ny, 128), V(nx + 2, ny, 128), V(6, nx, ny, 128), V(nx, ny, 128), V(nx, ny, 128), V(nx, ny, 128),
                V(2, nx, 128), V(2, 8, 128), V(5, 2, ny, 128), V(5, 2, nx, 128), V(5, 2, 8, 128)]

    X2, F2 = 8 * GX, 128 * GY * GZ
    X3, F3 = 4 * GX, max(128, 32 * GY * GZ)
    scratch = level(32, 16) + level(16, 8) + [
        V(32, 16, 128), V(32, 16, 128), V(16, 8, 128), V(32, 16, 128), V(16, 8, 128), V(16, 8, 128), V(16, 8, 128),
        V(256, 128), V(128, 128), V(64, 128),
        V(16, 128), V(8, 128), V(N, 16, 128), V(N, 8, 128),
        V(X2, F2), V(6, X2, F2), V(6, X3, F3), V(2, X2, F2), V(2, X3, F3),
        pltpu.SemaphoreType.DMA((10, 6)), pltpu.SemaphoreType.DMA((10, 6)), pltpu.SemaphoreType.DMA((4,))]
    vmem = pl.BlockSpec(memory_space=pltpu.VMEM)
    smem = pl.BlockSpec(memory_space=pltpu.SMEM)
    return pl.pallas_call(
        functools.partial(kernel, sizes),
        out_shape=jax.ShapeDtypeStruct(right_side.shape, f32),
        in_specs=[vmem, vmem, vmem, smem, smem],
        out_specs=vmem,
        scratch_shapes=scratch,
        compiler_params=pltpu.CompilerParams(has_side_effects=True, vmem_limit_bytes=56 * 2**20),
    )(right_side, phase_label, viscosity, mobility_table, shift_table)


def solution(mesh):
    sizes = tuple(mesh.shape[a] for a in ("gx", "gy", "gz"))
    in_specs = (P("gx", "gy", "gz"), P("gx", "gy", "gz"), P("gx", "gy", "gz"), P(), P())
    return jax.shard_map(functools.partial(body, sizes), mesh=mesh, in_specs=in_specs,
                         out_specs=P("gx", "gy", "gz"), check_vma=False)
```

time: 622 us -> 58 us (0.09)
  starting transfers between devices: 307 us -> 0 us
  waiting for transfers between devices: 126 us -> 0 us
  other arithmetic: 75.5 us -> 0 us
  local copies, waits for them, and re-layouts: 76.2 us -> 1.67 us
  Pallas kernels: 0 us -> 56.2 us
  blocking collectives: 27.8 us -> 0 us
    ppermute x120 -> x0, starting transfers between devices: 307 us -> none  [the longest x60 229 us: extended(): before = lax.ppermute(last, axis, up)]
    ppermute x120 -> x0, waiting for transfers between devices: 126 us -> none  [the longest x60 89.1 us: extended(): after = lax.ppermute(leading, axis, down)]
    reshape x13 -> x0, local copies, waits for them, and re-layouts: 60.8 us -> none  [the longest x7 59.8 us: block_sum(): return field.reshape(a // 2, 2, b // 2, 2, c // 2, 2).sum(axis=(1, 3, 5))]
    pallas_call x0 -> x1, Pallas kernels: none -> 56.2 us  [body(): pl.pallas_call(functools.partial(kernel, sizes), out_shape=jax.ShapeDtype...]
    reduce_sum x18 -> x0, other arithmetic: 28.8 us -> none  [block_sum(): return field.reshape(a // 2, 2, b // 2, 2, c // 2, 2).sum(axis=(1, 3, 5))]
    all_gather x3 -> x0, blocking collectives: 27.8 us -> none  [the longest x1 13.1 us: collected(): whole = lax.all_gather(stacked, 'gz', axis=3, tiled=True)]
    add x63 -> x0, other arithmetic: 23.5 us -> none  [the longest x12 18 us: cycle(): field = field + OMEGA * (rhs - remote_apply(field, terms, shift)) / diag]
    div x8 -> x0, other arithmetic: 6.23 us -> none  [the longest x4 5.52 us: cycle(): field = OMEGA * rhs / diag]
  transfers between devices with their start and end apart: 120 -> 0, of which waited for: 63 -> 0; matrix products, arithmetic and copies ran while one was open for 19% -> 0% of each run, Pallas kernels for 0% -> 0%
where the time goes in v1:
time: 58 us; the launch traced here: 57.8 us
  Pallas kernels  56.2 us (97%)
  local copies, waits for them, and re-layouts  1.67 us (3%)
    pallas_call x1, Pallas kernels, body(): pl.pallas_call(functools.partial(kernel, sizes), out_shape=jax.ShapeDtype...  56.2 us
    unnamed x1, local copies, waits for them, and re-layouts  1.67 us

profile of v1, /device:TPU:0, one launch (start us, length us, event | category | flops | bytes accessed | tf_op | source)
XLA Modules:
  0.0 57.8 jit_solution(6608738520507774874)
XLA Ops:
  0.0 56.2 %shard_map.55 = f32[32,16,128]{2,1,0:T(8,128)} custom-call(f32[32,16,128]{2,1,0:T(8,128)} %b_ref.1, s32[32,16,128]{2,1,0:T(8,128)} %ph_ref.1, f32[32,16,128]{2,1,0:T(8,128)} %visc_ref.1, f32[3]{0:T(128)} %mt_ref.1, f32[3]{0:T(128)} %st_ref.1), custom_call_target="tpu_custom_call" | custom-call | tf_op jit(solution)/shard_map/pallas_call | solution.py:444
  56.2 1.7 %copy.7 = f32[32,16,128]{2,1,0:T(8,128)} copy(f32[32,16,128]{2,1,0:T(8,128)} %shard_map.55) | data formatting | bytes 524288

commit v2 on v1

--- a/solution.py
+++ b/solution.py
@@ -209,21 +209,49 @@
             total = total + dot(both, place)
         return total
 
+    line = (ix * GY + iy) * GZ
+
+    def z_peer(step):
+        return (ix, iy, lax.rem(iz + step, GZ))
+
+    def plane_peer(step):
+        at = lax.rem(ix * GY + iy + step, GX * GY)
+        return (at // GY, lax.rem(at, GY), iz)
+
+    def each(count, fn):
+        if count <= 8:
+            for step in range(1, count):
+                fn(step)
+        else:
+            lax.fori_loop(1, count, lambda step, _: (fn(step), 0)[1], 0)
+
+    def greet(to):
+        pl.semaphore_signal(barrier, inc=1, device_id=to, device_id_type=MESH)
+
     def gather_start(src, dst, k):
-        def send(step, _):
-            peer = lax.rem(me + step, N)
-            to = (peer // (GY * GZ), lax.rem(peer // GZ, GY), lax.rem(peer, GZ))
+        def send(step):
             pltpu.make_async_remote_copy(
-                src_ref=src, dst_ref=dst.at[me], send_sem=gsem.at[2 * k], recv_sem=gsem.at[2 * k + 1],
-                device_id=to, device_id_type=MESH).start()
-            return 0
-        lax.fori_loop(1, N, send, 0)
+                src_ref=src, dst_ref=dst.at[me], send_sem=gsem.at[4 * k], recv_sem=gsem.at[4 * k + 1],
+                device_id=z_peer(step), device_id_type=MESH).start()
+        each(GZ, send)
+        dst[pl.ds(me, 1)] = src[...][None]
+
+    def gather_middle(src, dst, k):
+        rest = dst.at[pl.ds(0, GZ - 1)]
+        pltpu.make_async_copy(rest, rest, gsem.at[4 * k]).wait()
+        pltpu.make_async_copy(rest, rest, gsem.at[4 * k + 1]).wait()
+        lines = dst.at[pl.ds(line, GZ)]
+
+        def send(step):
+            pltpu.make_async_remote_copy(
+                src_ref=lines, dst_ref=lines, send_sem=gsem.at[4 * k + 2], recv_sem=gsem.at[4 * k + 3],
+                device_id=plane_peer(step), device_id_type=MESH).start()
+        each(GX * GY, send)
 
     def gather_finish(src, dst, k):
-        rest = dst.at[pl.ds(0, N - 1)]
-        pltpu.make_async_copy(rest, rest, gsem.at[2 * k]).wait()
-        pltpu.make_async_copy(rest, rest, gsem.at[2 * k + 1]).wait()
-        dst[pl.ds(me, 1)] = src[...][None]
+        rest = dst.at[pl.ds(0, N - GZ)]
+        pltpu.make_async_copy(rest, rest, gsem.at[4 * k + 2]).wait()
+        pltpu.make_async_copy(rest, rest, gsem.at[4 * k + 3]).wait()
 
     X2, Y2, Z2 = 8 * GX, 4 * GY, 32 * GZ
 
@@ -297,6 +325,10 @@
     d3 = (X2 // 2, Y2 // 2, Z2 // 2)
     d4 = (X2 // 4, Y2 // 4, Z2 // 4)
 
+    barrier = pltpu.get_barrier_semaphore()
+    each(GZ, lambda step: greet(z_peer(step)))
+    each(GX * GY, lambda step: greet(plane_peer(step)))
+
     sz0[...] = jnp.zeros(sz0.shape, jnp.float32)
     sz1[...] = jnp.zeros(sz1.shape, jnp.float32)
 
@@ -311,6 +343,7 @@
         xb0[pl.ds(1 + at, CHUNK)] = mob / visc_ref[pl.ds(at, CHUNK)]
         s0[pl.ds(at, CHUNK)] = shift
     chunks(L0, look_up)
+    pl.semaphore_wait(barrier, GZ - 1 + GX * GY - 1)
     start(L0, xb0, 0)
 
     lane1 = iota((16, 8, LANES), 2)
@@ -328,6 +361,7 @@
     start(L0, xa0, 1)
     finish(L1, xb1, 0)
     coefficients(L1, xb1, 0, s1)
+    gather_middle(pk_ms, g_ms, 0)
     finish(L0, xa0, 1)
     sweep(L0, xa0, 1, into(xb0))
     start(L0, xb0, 2)
@@ -361,6 +395,7 @@
     sweep(L1, xb1, 2, residual(L1, r1))
     pk_r[...] = pack(r1[...])
     gather_start(pk_r, g_r, 1)
+    gather_middle(pk_r, g_r, 1)
     gather_finish(pk_r, g_r, 1)
 
     base2 = unpack(lambda n: g_r[n]) * dj2[0]
@@ -438,7 +473,7 @@
         V(256, 128), V(128, 128), V(64, 128),
         V(16, 128), V(8, 128), V(N, 16, 128), V(N, 8, 128),
         V(X2, F2), V(6, X2, F2), V(6, X3, F3), V(2, X2, F2), V(2, X3, F3),
-        pltpu.SemaphoreType.DMA((10, 6)), pltpu.SemaphoreType.DMA((10, 6)), pltpu.SemaphoreType.DMA((4,))]
+        pltpu.SemaphoreType.DMA((10, 6)), pltpu.SemaphoreType.DMA((10, 6)), pltpu.SemaphoreType.DMA((8,))]
     vmem = pl.BlockSpec(memory_space=pltpu.VMEM)
     smem = pl.BlockSpec(memory_space=pltpu.SMEM)
     return pl.pallas_call(
@@ -447,7 +482,7 @@
         in_specs=[vmem, vmem, vmem, smem, smem],
         out_specs=vmem,
         scratch_shapes=scratch,
-        compiler_params=pltpu.CompilerParams(has_side_effects=True, vmem_limit_bytes=56 * 2**20),
+        compiler_params=pltpu.CompilerParams(has_side_effects=True, collective_id=0, vmem_limit_bytes=56 * 2**20),
     )(right_side, phase_label, viscosity, mobility_table, shift_table)
 
 

time: 58 us -> 54.2 us (0.934)
  Pallas kernels: 56.2 us -> 52.4 us
    pallas_call x1, Pallas kernels: 56.2 us -> 52.4 us  [body(): pl.pallas_call(functools.partial(kernel, sizes), out_shape=jax.ShapeDtype...]
where the time goes in v2:
time: 54.2 us; the launch traced here: 54 us
  Pallas kernels  52.4 us (97%)
  local copies, waits for them, and re-layouts  1.67 us (3%)
    pallas_call x1, Pallas kernels, body(): pl.pallas_call(functools.partial(kernel, sizes), out_shape=jax.ShapeDtype...  52.4 us
    unnamed x1, local copies, waits for them, and re-layouts  1.67 us

profile of v2, /device:TPU:0, one launch (start us, length us, event | category | flops | bytes accessed | tf_op | source)
XLA Modules:
  0.0 54.0 jit_solution(17715621320389347613)
XLA Ops:
  0.0 52.4 %shard_map.55 = f32[32,16,128]{2,1,0:T(8,128)} custom-call(f32[32,16,128]{2,1,0:T(8,128)} %b_ref.1, s32[32,16,128]{2,1,0:T(8,128)} %ph_ref.1, f32[32,16,128]{2,1,0:T(8,128)} %visc_ref.1, f32[3]{0:T(128)} %mt_ref.1, f32[3]{0:T(128)} %st_ref.1), custom_call_target="tpu_custom_call" | custom-call | tf_op jit(solution)/shard_map/pallas_call | solution.py:479
  52.4 1.7 %copy.7 = f32[32,16,128]{2,1,0:T(8,128)} copy(f32[32,16,128]{2,1,0:T(8,128)} %shard_map.55) | data formatting | bytes 524288

commit v3 on v2

--- a/solution.py
+++ b/solution.py
@@ -14,8 +14,24 @@
 MESH = pl.DeviceIdType.MESH
 
 
-def dot(a, b):
-    return jnp.dot(a, b, precision=lax.Precision.HIGHEST, preferred_element_type=jnp.float32)
+def parts(v):
+    high = v.astype(jnp.bfloat16)
+    left = v - high.astype(jnp.float32)
+    middle = left.astype(jnp.bfloat16)
+    low = (left - middle.astype(jnp.float32)).astype(jnp.bfloat16)
+    return high, middle, low
+
+
+def dot(a, place):
+    place = place.astype(jnp.bfloat16)
+    high, middle, low = [jnp.dot(p, place, preferred_element_type=jnp.float32) for p in parts(a)]
+    return high + (middle + low)
+
+
+def left_dot(place, b):
+    place = place.astype(jnp.bfloat16)
+    high, middle, low = [jnp.dot(place, p, preferred_element_type=jnp.float32) for p in parts(b)]
+    return high + (middle + low)
 
 
 def iota(shape, dim):
@@ -26,14 +42,22 @@
     return jnp.where(mask, 1.0, 0.0).astype(jnp.float32)
 
 
+def over(i, n):
+    return i >> (n.bit_length() - 1) if n & (n - 1) == 0 else i // n
+
+
+def rest(i, n):
+    return i & (n - 1) if n & (n - 1) == 0 else i % n
+
+
 def pair_lanes(fine, coarse, zf, zc):
     i, j = iota((fine, coarse), 0), iota((fine, coarse), 1)
-    return ones_where(((i // zf) // 2 == j // zc) & ((i % zf) // 2 == j % zc))
+    return ones_where(((over(i, zf) >> 1) == over(j, zc)) & ((rest(i, zf) >> 1) == rest(j, zc)))
 
 
 def pair_lanes_back(coarse, fine, zf, zc):
     j, i = iota((coarse, fine), 0), iota((coarse, fine), 1)
-    return ones_where(((i // zf) // 2 == j // zc) & ((i % zf) // 2 == j % zc))
+    return ones_where(((over(i, zf) >> 1) == over(j, zc)) & ((rest(i, zf) >> 1) == rest(j, zc)))
 
 
 def kernel(sizes, b_ref, ph_ref, visc_ref, mt_ref, st_ref, out_ref,
@@ -237,9 +261,9 @@
         dst[pl.ds(me, 1)] = src[...][None]
 
     def gather_middle(src, dst, k):
-        rest = dst.at[pl.ds(0, GZ - 1)]
-        pltpu.make_async_copy(rest, rest, gsem.at[4 * k]).wait()
-        pltpu.make_async_copy(rest, rest, gsem.at[4 * k + 1]).wait()
+        part = dst.at[pl.ds(0, GZ - 1)]
+        pltpu.make_async_copy(part, part, gsem.at[4 * k]).wait()
+        pltpu.make_async_copy(part, part, gsem.at[4 * k + 1]).wait()
         lines = dst.at[pl.ds(line, GZ)]
 
         def send(step):
@@ -249,9 +273,9 @@
         each(GX * GY, send)
 
     def gather_finish(src, dst, k):
-        rest = dst.at[pl.ds(0, N - GZ)]
-        pltpu.make_async_copy(rest, rest, gsem.at[4 * k + 2]).wait()
-        pltpu.make_async_copy(rest, rest, gsem.at[4 * k + 3]).wait()
+        part = dst.at[pl.ds(0, N - GZ)]
+        pltpu.make_async_copy(part, part, gsem.at[4 * k + 2]).wait()
+        pltpu.make_async_copy(part, part, gsem.at[4 * k + 3]).wait()
 
     X2, Y2, Z2 = 8 * GX, 4 * GY, 32 * GZ
 
@@ -268,7 +292,7 @@
                         v = read((gx * GY + gy) * GZ + 4 * t + p)
                         shift = (32 * (p - q)) % LANES
                         v = pltpu.roll(v, shift, 1) if shift else v
-                        tile = jnp.where(lane // 32 == p, v, tile)
+                        tile = jnp.where((lane >> 5) == p, v, tile)
                     tiles.append(tile)
             rows.append(jnp.concatenate(tiles, axis=1))
         return jnp.concatenate(rows, axis=0)
@@ -279,7 +303,7 @@
         row, lane = iota(shape, 0), iota(shape, 1)
         width = shape[1]
         valid = lane < Y * Z
-        z, y = lane % Z, lane // Z
+        z, y = rest(lane, Z), over(lane, Z)
         inside = [row < X - 1, row > 0, y < Y - 1, y > 0, z < Z - 1, z > 0]
         diag = s
         terms = []
@@ -310,13 +334,13 @@
         tiles = [dot(r[:, k * span:(k + 1) * span], place) for k in range(Y * Z // span)]
         wide = jnp.concatenate(tiles, axis=1) if len(tiles) > 1 else tiles[0]
         left = ones_where(iota((X // 2, X), 1) // 2 == iota((X // 2, X), 0))
-        return dot(left, wide)
+        return left_dot(left, wide)
 
     def flat_spread(e, dims):
         X, Y, Z = dims
         span = min(4 * LANES, Y * Z)
         left = ones_where(iota((X, X // 2), 0) // 2 == iota((X, X // 2), 1))
-        tall = dot(left, e)
+        tall = left_dot(left, e)
         place = pair_lanes_back(LANES, span, Z, Z // 2)
         tiles = [dot(tall[:, k * LANES:(k + 1) * LANES], place) for k in range(Y * Z // span)]
         return jnp.concatenate(tiles, axis=1) if len(tiles) > 1 else tiles[0]
@@ -375,22 +399,22 @@
     dj2[0], dj2[1] = inv, dg
     m3 = flat_restrict(m2, d2) * 0.25
     s3 = flat_restrict(s2, d2)
+
+    finish(L0, xb0, 2)
+    sweep(L0, xb0, 2, residual(L0, r0))
+    r1[...] = restrict0(lambda c: r0[16 * c:16 + 16 * c])
+    begin(L1, r1, xa1)
+    start(L1, xa1, 1)
     w, inv, dg = flat_terms(m3, s3, d3)
     for d in range(6):
         wj3[d] = w[d]
     dj3[0], dj3[1] = inv, dg
     m4 = flat_restrict(m3, d3) * 0.25
     s4 = flat_restrict(s3, d3)
-    w4, inv4, _ = flat_terms(m4, s4, d4)
-
-    finish(L0, xb0, 2)
-    sweep(L0, xb0, 2, residual(L0, r0))
-    r1[...] = restrict0(lambda c: r0[16 * c:16 + 16 * c])
-    begin(L1, r1, xa1)
-    start(L1, xa1, 1)
     finish(L1, xa1, 1)
     sweep(L1, xa1, 1, into(xb1))
     start(L1, xb1, 2)
+    w4, inv4, _ = flat_terms(m4, s4, d4)
     finish(L1, xb1, 2)
     sweep(L1, xb1, 2, residual(L1, r1))
     pk_r[...] = pack(r1[...])

time: 54.2 us -> 53.6 us (0.989)
  Pallas kernels: 52.4 us -> 51.8 us
    pallas_call x1, Pallas kernels: 52.4 us -> 51.8 us  [body(): pl.pallas_call(functools.partial(kernel, sizes), out_shape=jax.ShapeDtype...]
where the time goes in v3:
time: 53.6 us; the launch traced here: 53.5 us
  Pallas kernels  51.8 us (97%)
  local copies, waits for them, and re-layouts  1.67 us (3%)
    pallas_call x1, Pallas kernels, body(): pl.pallas_call(functools.partial(kernel, sizes), out_shape=jax.ShapeDtype...  51.8 us
    unnamed x1, local copies, waits for them, and re-layouts  1.67 us

profile of v3, /device:TPU:0, one launch (start us, length us, event | category | flops | bytes accessed | tf_op | source)
XLA Modules:
  0.0 53.5 jit_solution(2637267406278282654)
XLA Ops:
  0.0 51.8 %shard_map.55 = f32[32,16,128]{2,1,0:T(8,128)} custom-call(f32[32,16,128]{2,1,0:T(8,128)} %b_ref.1, s32[32,16,128]{2,1,0:T(8,128)} %ph_ref.1, f32[32,16,128]{2,1,0:T(8,128)} %visc_ref.1, f32[3]{0:T(128)} %mt_ref.1, f32[3]{0:T(128)} %st_ref.1), custom_call_target="tpu_custom_call" | custom-call | tf_op jit(solution)/shard_map/pallas_call | solution.py:503
  51.8 1.7 %copy.7 = f32[32,16,128]{2,1,0:T(8,128)} copy(f32[32,16,128]{2,1,0:T(8,128)} %shard_map.55) | data formatting | bytes 524288
